TPU v7x, 128 devices: a whole 4x4x4 slice. The times are simulated.
128 devices in a mesh: grp: 4 (over x_hi, core), tile: 32 (over y, x_lo, z).
Axes of the slice: x: 4 (x_hi: 2, x_lo: 2; x = x_hi * 2 + x_lo), y: 4, z: 4, core: 2. Of those that a mesh axis runs over, the one named last changes fastest.
Arguments:
- soil_head: float32 [8, 1024, 4096], P(None, 'grp', 'tile'), may hold values from -2 to 0.5
- soil_type: int32 [8, 1024, 4096], P(None, 'grp', 'tile'), may hold values from 0 to 11
- soil_table: float32 [3, 12], replicated, may hold values from 0.2 to 2
- emitter_cell: int32 [4, 32, 64], P('grp', 'tile'), may hold values from 0 to 262143
- emitter_rate: float32 [4, 32, 64], P('grp', 'tile'), may hold values from 0.5 to 2
- pond_depth: float32 [1024, 4096], P(('grp', 'tile')), may hold values from 0 to 0.5
- elevation: float32 [1024, 4096], P(('grp', 'tile')), may hold values from 0 to 2
- roughness: float32 [1024, 4096], P(('grp', 'tile')), may hold values from 0.2 to 5
- ponding: int32 [1024, 4096], P(('grp', 'tile')), may hold values 0 or 1
- rain_rate: float32 [1024, 4096], P(('grp', 'tile')), may hold values from 0 to 0.5
Outputs:
- head_next: float32 [8, 1024, 4096], P(None, 'grp', 'tile')
- depth_next: float32 [1024, 4096], P(('grp', 'tile'))
Inputs may be any that keep to these rules, and one draw needn't show every extreme that they name: `emitter_cell`: each entry is layer * 256 * 128 + row * 128 + column of a cell in the owning device's block.
All inputs are finite; a program needn't handle non-finite values. No bound on the sum of `ponding` on one device may be relied on, other than what follows from the above.
Results may differ from a plain program's by a relative error of at most 0.00002.
Values sent between devices are 32-bit elements; how exact they have to be, the bound alone decides.
A program may use at most 128 MiB of HBM per device.

v0:
```python
import jax
import jax.numpy as jnp
from jax import lax
from jax.experimental import pallas as pl
from jax.experimental.pallas import tpu as pltpu
from jax.sharding import PartitionSpec as P

MESH = pl.DeviceIdType.MESH
STEPS = 2
PICARD = 2
ROUNDS = STEPS * PICARD
LANES = 128
STORAGE = 0.05
FILM_FLOOR = 0.04
BLEND = 0.05
LOG2E = 1.4426950408889634
OUTSIDE = 1e-30
PLANES = 8
WS, WD = 2, 3
H, SAT, SHP, CAP, EM = 0, 2, 3, 4, 5
SIDES = ((0, -1), (0, 1), (-1, 0), (1, 0), (1, 1), (1, -1), (-1, 1), (-1, -1))


def inverse(x):
    r = pl.reciprocal(x, approx=True)
    return r * (2.0 - x * r)


def face_of(a, b):
    return (a + a) * b * inverse(a + b)


def film_face(a, b):
    return (a + a) * b * inverse(a + b + BLEND)


def roll(x, shift):
    return pltpu.roll(x, shift % LANES, 1)


def make_kernel(n_grp, n_tile, layers, rows, n_types, n_emit):
    XI = rows // 8
    RP = XI + 16
    ZP = (PLANES + 2 * WS) * RP
    SP = (PLANES + 2 * WD) * RP
    nq = XI // 8
    top = layers - 1
    N = XI + 8
    yv = (WD * nq + 7) // 8

    def kernel(
        head_in, type_in, table, cell, rate, depth_in, elev_in, rough_in, pond_in, rain_in,
        head_out, depth_out,
        BIG, G1, K, FX, FY, FZ, RD, B, C, NAT, TYPE,
        A_SEND, A_RECV, ROUGH, POND, DN,
        SF, FILM, ETA, ETA2, GX, GY, SB, SRD,
        YS, YR, XS, XR, CS, CR, TYS, TYR, TXS, TXR, TCS, TCR,
        load_sem, a_send, a_recv, o_send, o_recv, out_sem,
        c_send, c_recv, t_send, t_recv,
    ):
        g = lax.axis_index("grp")
        t = lax.axis_index("tile")

        def inside(dg, dt):
            ok = jnp.bool_(True)
            if dg:
                ok = g + dg >= 0 if dg < 0 else g + dg < n_grp
            if dt:
                side = t + dt >= 0 if dt < 0 else t + dt < n_tile
                ok = jnp.logical_and(ok, side) if dg else side
            return ok

        has = [inside(dg, dt) for dg, dt in SIDES]
        came = [inside(-dg, -dt) for dg, dt in SIDES]
        target = [(g + dg, t + dt) for dg, dt in SIDES]

        loads = [
            pltpu.make_async_copy(rough_in, ROUGH, load_sem.at[0]),
            pltpu.make_async_copy(pond_in, POND, load_sem.at[1]),
            pltpu.make_async_copy(depth_in, A_SEND.at[0], load_sem.at[2]),
            pltpu.make_async_copy(elev_in, A_SEND.at[1], load_sem.at[3]),
            pltpu.make_async_copy(rain_in, A_SEND.at[3], load_sem.at[4]),
            pltpu.make_async_copy(type_in, TYPE, load_sem.at[5]),
            pltpu.make_async_copy(head_in, NAT, load_sem.at[6]),
        ]
        for copy in loads:
            copy.start()

        barrier = pltpu.get_barrier_semaphore()

        @pl.loop(1, n_tile)
        def _(d):
            pl.semaphore_signal(
                barrier, inc=1, device_id=(g, lax.rem(t + d, n_tile)), device_id_type=MESH
            )

        for side in range(2, 8):

            @pl.when(has[side])
            def _():
                pl.semaphore_signal(barrier, inc=1, device_id=target[side], device_id_type=MESH)

        lane = lax.broadcasted_iota(jnp.int32, (8, LANES), 1)
        xb = lax.bitwise_and(lane, 7)
        zero8 = jnp.zeros((8, LANES), jnp.float32)

        @pl.loop(0, ZP // 8)
        def _(r):
            for base in (0, (layers + 1) * ZP):
                at = pl.ds(pl.multiple_of(base + r * 8, 8), 8)
                BIG[H, at, :] = zero8
                BIG[H + 1, at, :] = zero8
                G1[at, :] = zero8
                K[at, :] = zero8
            FZ[pl.ds(pl.multiple_of(r * 8, 8), 8), :] = zero8

        for side in range(8):

            @pl.when(jnp.logical_not(came[side]))
            def _():
                for k in range(5 + ROUNDS - 1):
                    fill = zero8 + OUTSIDE if k == 1 else zero8
                    if side < 2:
                        for z in range(layers):
                            YR[side, k, z] = fill
                    elif side < 4:
                        for v in range(4):
                            XR[side - 2, k, v] = fill
                    else:
                        CR[side - 4, k] = fill
                for k in range(4 + ROUNDS - 1):
                    if side < 2:
                        for v in range(yv):
                            TYR[side, k, v] = zero8
                    elif side < 4:
                        TXR[side - 2, k] = zero8
                    else:
                        TCR[side - 4, k] = zero8

        for copy in loads[:5]:
            copy.wait()
        A_SEND[2] = ROUGH[...] * POND[...].astype(jnp.float32)
        own = pltpu.make_async_copy(
            A_SEND.at[:, :, pl.ds(pl.multiple_of(t * LANES, LANES), LANES)],
            A_RECV.at[:, pl.ds(pl.multiple_of(t * 8, 8), 8), :],
            a_recv,
        )
        own.start()

        beside = jnp.int32(0)
        for side in range(2, 8):
            beside = beside + came[side].astype(jnp.int32)
        pl.semaphore_wait(barrier, n_tile - 1 + beside)

        @pl.loop(1, n_tile)
        def _(d):
            peer = lax.rem(t + d, n_tile)
            pltpu.make_async_remote_copy(
                src_ref=A_SEND.at[:, :, pl.ds(pl.multiple_of(peer * LANES, LANES), LANES)],
                dst_ref=A_RECV.at[:, pl.ds(pl.multiple_of(t * 8, 8), 8), :],
                send_sem=a_send,
                recv_sem=a_recv,
                device_id=(g, peer),
                device_id_type=MESH,
            ).start()

        def copies(bufs, k, count, send, recv):
            y_out, y_in, x_out, x_in, c_out, c_in = bufs
            at = pl.ds(k, count)
            out = []
            for side in range(8):
                if side < 2:
                    src, dst = y_out.at[at], y_in.at[side, at]
                elif side < 4:
                    src, dst = x_out.at[at], x_in.at[side - 2, at]
                else:
                    src, dst = c_out.at[side - 4, at], c_in.at[side - 4, at]
                out.append(
                    pltpu.make_async_remote_copy(
                        src_ref=src,
                        dst_ref=dst,
                        send_sem=send.at[side],
                        recv_sem=recv.at[side],
                        device_id=target[side],
                        device_id_type=MESH,
                    )
                )
            return out

        soil_bufs = (YS, YR, XS, XR, CS, CR)
        surface_bufs = (TYS, TYR, TXS, TXR, TCS, TCR)

        def soil_copies(e):
            if isinstance(e, int) and e == 0:
                return copies(soil_bufs, 0, 5, c_send.at[0], c_recv.at[0])
            return copies(soil_bufs, 4 + e, 1, c_send.at[e], c_recv.at[e])

        def surface_copies(e):
            if isinstance(e, int) and e == 0:
                return copies(surface_bufs, 0, 4, t_send.at[0], t_recv.at[0])
            return copies(surface_bufs, 3 + e, 1, t_send.at[e], t_recv.at[e])

        def start(made):
            for side in (1, 0, 4, 5, 6, 7, 2, 3):

                @pl.when(has[side])
                def _():
                    made[side].start()

        def wait_recv(made):
            for side in range(8):

                @pl.when(came[side])
                def _():
                    made[side].wait_recv()

        def wait_send(made):
            for side in range(8):

                @pl.when(has[side])
                def _():
                    made[side].wait_send()

        def fold(v):
            v = list(v)
            for k in (1, 2, 4):
                low = lax.bitwise_and(lane, k) == 0
                for a in range(8):
                    if a & k == 0:
                        p, q = v[a], v[a | k]
                        v[a] = jnp.where(low, p, roll(q, k))
                        v[a | k] = jnp.where(low, roll(p, -k), q)
            return v

        def soil_row(plane, xi):
            return (plane + WS) * RP + 8 + xi

        def film_row(plane, xi):
            return (plane + WD) * RP + 8 + xi

        def columns_out(R, base, row, width, put):
            packed = zero8
            for a in range(1, width + 1):
                for q in range(nq):
                    i = (a - 1) * nq + q
                    high = roll(R[pl.ds(base + row(PLANES - a, 8 * q), 8), :], 8)
                    low = roll(R[pl.ds(base + row(a - 1, 8 * q), 8), :], -8)
                    R[pl.ds(base + row(-a, 8 * q), 8), :] = high
                    R[pl.ds(base + row(PLANES - 1 + a, 8 * q), 8), :] = low
                    both = jnp.where(lane >= LANES // 2, low, high)
                    slot = i % 8
                    moved = roll(both, 16 * slot + 8)
                    packed = jnp.where(lax.shift_right_logical(lane, 4) == slot, moved, packed)
                    if slot == 7 or i == width * nq - 1:
                        put(i // 8, packed)
                        packed = zero8

        def columns_in(R, base, row, width, get):
            for a in range(1, width + 1):
                for q in range(nq):
                    i = (a - 1) * nq + q
                    if i % 8 == 0:
                        from_right, from_left = get(i // 8)
                        met = jnp.where(lax.bitwise_and(lane, 15) < 8, from_right, from_left)
                    u = roll(met, -(16 * (i % 8) + 8))
                    at = pl.ds(base + row(-a, 8 * q), 8)
                    R[at, :] = jnp.where(lane < 8, u, R[at, :])
                    at = pl.ds(base + row(PLANES - 1 + a, 8 * q), 8)
                    R[at, :] = jnp.where(lane >= LANES - 8, u, R[at, :])

        def rows_out(R, base, row, b, slot, packed):
            high = roll(R[pl.ds(base + row(0, XI - b), 8, stride=RP), :], 1)
            low = roll(R[pl.ds(base + row(0, b - 1), 8, stride=RP), :], -1)
            R[pl.ds(base + row(0, -b), 8, stride=RP), :] = high
            R[pl.ds(base + row(0, XI - 1 + b), 8, stride=RP), :] = low
            both = jnp.where(xb == 7, low, high)
            mine = lax.shift_right_logical(xb, 1) == slot
            return jnp.where(mine, roll(both, 2 * slot + 1), packed)

        def rows_meet(from_down, from_up):
            return jnp.where(lax.bitwise_and(lane, 1) == 1, roll(from_up, -8), roll(from_down, 8))

        def rows_in(R, base, row, b, slot, met):
            u = roll(met, -(2 * slot + 1))
            at = pl.ds(base + row(0, -b), 8, stride=RP)
            R[at, :] = jnp.where(xb == 0, u, R[at, :])
            at = pl.ds(base + row(0, XI - 1 + b), 8, stride=RP)
            R[at, :] = jnp.where(xb == 7, u, R[at, :])

        def corner_source(gather, side, a, b):
            plane = PLANES - a if side in (4, 6) else a - 1
            xi = XI - b if side in (4, 5) else b - 1
            return roll(gather(plane, xi), {4: 1, 5: 113, 6: 15, 7: 127}[side])

        def corner_value(gather, side, a, b, diagonal):
            ln = lane[: diagonal.shape[0]]
            x8 = xb[: diagonal.shape[0]]
            first = side in (4, 6)
            plane = -a if first else PLANES - 1 + a
            if side in (4, 5):
                inner = roll(gather(plane, XI - b), 1)
                other = gather(PLANES - a if first else a - 1, -b)
                near = x8 > 0
            else:
                inner = roll(gather(plane, b - 1), -1)
                other = gather(PLANES - a if first else a - 1, XI - 1 + b)
                near = x8 < 7
            other = roll(other, 8 if first else -8)
            known = ln >= 8 if first else ln < LANES - 8
            return jnp.where(near, inner, jnp.where(known, other, diagonal))

        def corner_place(side, a, b):
            return -a if side in (4, 6) else PLANES - 1 + a, -b if side in (4, 5) else XI - 1 + b

        def soil_out(f, k):
            R = BIG.at[f]

            @pl.loop(0, layers)
            def _(z):
                base = pl.multiple_of((z + 1) * ZP, 8)

                def put(v, value):
                    YS[k, z] = value

                columns_out(R, base, soil_row, WS, put)

            packs = [zero8] * 4
            for z in range(layers):
                for b in range(1, WS + 1):
                    v = (b - 1) * 2 + z // 4
                    packs[v] = rows_out(R, (z + 1) * ZP, soil_row, b, z % 4, packs[v])
            for v in range(4):
                XS[k, v] = packs[v]

            def gather(plane, xi):
                return R[pl.ds(ZP + soil_row(plane, xi), layers, stride=ZP), :]

            for side in range(4, 8):
                CS[side - 4, k] = corner_source(gather, side, 1, 1)

        def soil_in(f, k):
            R = BIG.at[f]

            @pl.loop(0, layers)
            def _(z):
                base = pl.multiple_of((z + 1) * ZP, 8)
                columns_in(R, base, soil_row, WS, lambda v: (YR[0, k, z], YR[1, k, z]))

            met = [rows_meet(XR[0, k, v], XR[1, k, v]) for v in range(4)]
            for z in range(layers):
                for b in range(1, WS + 1):
                    rows_in(R, (z + 1) * ZP, soil_row, b, z % 4, met[(b - 1) * 2 + z // 4])

            def gather(plane, xi):
                return R[pl.ds(ZP + soil_row(plane, xi), layers, stride=ZP), :]

            for side in range(4, 8):
                value = corner_value(gather, side, 1, 1, CR[side - 4, k])
                plane, xi = corner_place(side, 1, 1)
                R[pl.ds(ZP + soil_row(plane, xi), layers, stride=ZP), :] = value

        corners = ((1, 1), (1, 2), (2, 1))

        def surface_out(f, k):
            R = SF.at[f]

            def put(v, value):
                TYS[k, v] = value

            columns_out(R, 0, film_row, WD, put)
            packed = zero8
            for b in range(1, WD + 1):
                packed = rows_out(R, 0, film_row, b, b - 1, packed)
            TXS[k] = packed

            def gather(plane, xi):
                return R[pl.ds(film_row(plane, xi), 1), :]

            for side in range(4, 8):
                for n, (a, b) in enumerate(corners):
                    TCS[side - 4, k, pl.ds(n, 1), :] = corner_source(gather, side, a, b)

        def surface_in(f, k):
            R = SF.at[f]
            columns_in(R, 0, film_row, WD, lambda v: (TYR[0, k, v], TYR[1, k, v]))
            met = rows_meet(TXR[0, k], TXR[1, k])
            for b in range(1, WD + 1):
                rows_in(R, 0, film_row, b, b - 1, met)

            def gather(plane, xi):
                return R[pl.ds(film_row(plane, xi), 1), :]

            for side in range(4, 8):
                for n, (a, b) in enumerate(corners):
                    value = corner_value(gather, side, a, b, TCR[side - 4, k, pl.ds(n, 1), :])
                    plane, xi = corner_place(side, a, b)
                    R[pl.ds(film_row(plane, xi), 1), :] = value

        @pl.loop(0, 4 + ROUNDS - 1)
        def _(k):
            for side in range(4):
                TCS[side, k] = zero8

        loads[5].wait()
        loads[6].wait()

        @pl.loop(0, layers)
        def _(z):
            base = (z + 1) * ZP
            for q in range(nq):
                kinds = fold(
                    [TYPE[z, pl.ds(i * XI + 8 * q, 8), :].astype(jnp.float32) for i in range(8)]
                )
                heads = fold([NAT[z, pl.ds(i * XI + 8 * q, 8), :] for i in range(8)])
                for plane in range(PLANES):
                    at = pl.ds(pl.multiple_of(base + soil_row(plane, 8 * q), 8), 8)
                    sat = shp = cap = zero8
                    for c in range(n_types):
                        same = kinds[plane] == float(c)
                        sat = jnp.where(same, table[0, c], sat)
                        shp = jnp.where(same, table[1, c] * LOG2E, shp)
                        cap = jnp.where(same, table[2, c], cap)
                    BIG[SAT, at, :] = sat
                    BIG[SHP, at, :] = shp
                    BIG[CAP, at, :] = cap
                    BIG[H, at, :] = heads[plane]

        ids = jnp.broadcast_to(cell[0], (LANES, n_emit))
        amount = jnp.broadcast_to(rate[0], (LANES, n_emit))
        column = lax.bitwise_and(ids, LANES - 1)
        line = lax.rem(lax.shift_right_logical(ids, 7), rows)
        layer = lax.div(lax.shift_right_logical(ids, 7), rows)
        wanted_lane = lax.bitwise_and(column, LANES - 8) + lax.div(line, XI)
        plane_row = lax.bitwise_and(column, 7) * XI + lax.rem(line, XI) + layer * rows
        here = wanted_lane == lax.broadcasted_iota(jnp.int32, (LANES, n_emit), 0)
        picked = jnp.where(here, amount, 0.0)
        part0 = picked.astype(jnp.bfloat16)
        rest = picked - part0.astype(jnp.float32)
        part1 = rest.astype(jnp.bfloat16)
        part2 = (rest - part1.astype(jnp.float32)).astype(jnp.bfloat16)

        @pl.loop(0, layers)
        def _(z):
            size = min(LANES, rows)
            for r in range(0, rows, size):
                wanted = lax.broadcasted_iota(jnp.int32, (size, n_emit), 0) + (z * rows + r)
                hot = jnp.where(plane_row[:size] == wanted, 1.0, 0.0).astype(jnp.bfloat16)
                total = jnp.zeros((size, LANES), jnp.float32)
                for part in (part2, part1, part0):
                    total = total + lax.dot_general(
                        hot, part, (((1,), (1,)), ((), ())), preferred_element_type=jnp.float32
                    )
                for s in range(0, size, XI):
                    plane = (r + s) // XI
                    at = pl.multiple_of((z + 1) * ZP + soil_row(plane, 0), 8)
                    BIG[EM, pl.ds(at, XI), :] = total[s : s + XI]

        @pl.loop(0, 5)
        def _(k):
            soil_out(jnp.where(k == 0, 0, k + 1), k)

        start(soil_copies(0))

        pltpu.make_async_copy(A_RECV, A_RECV, a_recv).wait()

        @pl.loop(0, 4)
        def _(n):
            field = jnp.where(n == 0, 0, n + 1)
            for q in range(nq):
                parts = fold([A_RECV[n, pl.ds(i * XI + 8 * q, 8), :] for i in range(8)])
                for plane in range(PLANES):
                    SF[field, pl.ds(film_row(plane, 8 * q), 8), :] = parts[plane]

        D, ELEV, GAIN, RAIN = 0, 2, 3, 4

        @pl.loop(0, 4)
        def _(k):
            surface_out(jnp.where(k == 0, 0, k + 1), k)

        start(surface_copies(0))
        wait_recv(soil_copies(0))

        @pl.loop(0, 5)
        def _(k):
            soil_in(jnp.where(k == 0, 0, k + 1), k)

        wait_recv(surface_copies(0))

        @pl.loop(0, 4)
        def _(k):
            surface_in(jnp.where(k == 0, 0, k + 1), k)

        def zbase(z):
            return pl.multiple_of((z + 1) * ZP, 8)

        @pl.loop(0, ROUNDS)
        def _(p):
            slot = lax.rem(p, 2)
            other = 1 - slot
            src = BIG.at[slot]
            dst = BIG.at[other]
            depth = SF.at[slot]

            @pl.when(p > 0)
            def _():
                wait_recv(soil_copies(p))
                soil_in(slot, 4 + p)
                wait_recv(surface_copies(p))
                surface_in(slot, 3 + p)

            @pl.loop(0, layers)
            def _(z):
                base = zbase(z)
                for plane in range(-2, PLANES + 2):
                    at = pl.ds(base + soil_row(plane, -2), N)
                    grow = jnp.exp2(BIG[SHP, at, :] * jnp.minimum(src[at, :], 0.0))
                    K[at, :] = BIG[SAT, at, :] * grow
                    if -2 < plane < PLANES + 1:
                        store = BIG[CAP, at, :] * grow + STORAGE
                        C[at, :] = store
                        B[at, :] = store * BIG[H, at, :] + BIG[EM, at, :]

            for plane in range(-3, PLANES + 3):
                at = pl.ds(film_row(plane, -3), N)
                d = depth[at, :]
                square = d * d + FILM_FLOOR
                FILM[at, :] = SF[GAIN, at, :] * (square * lax.rsqrt(square))
                ETA[at, :] = SF[ELEV, at, :] + d
            for plane in range(-3, PLANES + 2):
                at = pl.ds(film_row(plane, -3), N)
                film = FILM[at, :]
                GX[at, :] = film_face(film, FILM[pl.ds(film_row(plane, -2), N), :])
                GY[at, :] = film_face(film, FILM[pl.ds(film_row(plane + 1, -3), N), :])

            def film_sum(source, plane, first):
                at = pl.ds(film_row(plane, first), N)
                after = pl.ds(film_row(plane, first + 1), N)
                before = pl.ds(film_row(plane, first - 1), N)
                right = pl.ds(film_row(plane + 1, first), N)
                left = pl.ds(film_row(plane - 1, first), N)
                return (
                    SB[at, :]
                    + GX[at, :] * source[after, :]
                    + GX[before, :] * source[before, :]
                    + GY[at, :] * source[right, :]
                    + GY[left, :] * source[left, :]
                ) * SRD[at, :]

            high = (top + 1) * ZP
            for plane in range(-2, PLANES + 2):
                at = pl.ds(film_row(plane, -2), N)
                soil_at = pl.ds(high + soil_row(plane, -2), N)
                faces = (
                    GX[at, :]
                    + GX[pl.ds(film_row(plane, -3), N), :]
                    + GY[at, :]
                    + GY[pl.ds(film_row(plane - 1, -2), N), :]
                )
                cond = K[soil_at, :]
                start_level = SF[D, at, :] + SF[RAIN, at, :] + cond * src[soil_at, :]
                SB[at, :] = start_level - faces * SF[ELEV, at, :]
                SRD[at, :] = inverse(1.0 + cond + faces)
                ETA2[at, :] = film_sum(ETA, plane, -2) + SF[ELEV, at, :]
            for plane in range(-1, PLANES + 1):
                at = pl.ds(film_row(plane, -1), N)
                soil_at = pl.ds(high + soil_row(plane, -1), N)
                d = film_sum(ETA2, plane, -1)
                SF[other, at, :] = d
                B[soil_at, :] = B[soil_at, :] + K[soil_at, :] * (d - src[soil_at, :])

            @pl.when(p < ROUNDS - 1)
            def _():
                surface_out(other, 4 + p)
                start(surface_copies(p + 1))

            @pl.when(p == ROUNDS - 1)
            def _():
                for q in range(nq):
                    parts = fold([SF[D, pl.ds(film_row(i, 8 * q), 8), :] for i in range(8)])
                    for i in range(8):
                        DN[pl.ds(i * XI + 8 * q, 8), :] = parts[i]
                pltpu.make_async_copy(
                    DN.at[pl.ds(pl.multiple_of(t * 8, 8), 8), :],
                    depth_out.at[:, pl.ds(pl.multiple_of(t * LANES, LANES), LANES)],
                    o_recv,
                ).start()

                @pl.loop(1, n_tile)
                def _(d):
                    peer = lax.rem(t + d, n_tile)
                    pltpu.make_async_remote_copy(
                        src_ref=DN.at[pl.ds(pl.multiple_of(peer * 8, 8), 8), :],
                        dst_ref=depth_out.at[:, pl.ds(pl.multiple_of(t * LANES, LANES), LANES)],
                        send_sem=o_send,
                        recv_sem=o_recv,
                        device_id=(g, peer),
                        device_id_type=MESH,
                    ).start()

            @pl.loop(0, layers)
            def _(z):
                base = zbase(z)
                for plane in range(-2, PLANES + 1):
                    at = pl.ds(base + soil_row(plane, -1), N)
                    k = K[at, :]
                    FY[at, :] = face_of(k, K[pl.ds(base + soil_row(plane + 1, -1), N), :])
                    if plane > -2:
                        FZ[at, :] = face_of(k, K[pl.ds(base + ZP + soil_row(plane, -1), N), :])
                        before = pl.ds(base + soil_row(plane, -2), N)
                        FX[before, :] = face_of(K[before, :], k)

            def soil_sum(source, base, plane, first, size, at, value, below, above):
                after = pl.ds(base + soil_row(plane, first + 1), size)
                before = pl.ds(base + soil_row(plane, first - 1), size)
                right = pl.ds(base + soil_row(plane + 1, first), size)
                left = pl.ds(base + soil_row(plane - 1, first), size)
                return (
                    value
                    + FX[at, :] * source[after, :]
                    + FX[before, :] * source[before, :]
                    + FY[at, :] * source[right, :]
                    + FY[left, :] * source[left, :]
                    + above * source[pl.ds(base + ZP + soil_row(plane, first), size), :]
                    + below * source[pl.ds(base - ZP + soil_row(plane, first), size), :]
                )

            @pl.loop(0, layers)
            def _(z):
                base = zbase(z)
                for plane in range(-1, PLANES + 1):
                    at = pl.ds(base + soil_row(plane, -1), N)
                    below = FZ[pl.ds(base - ZP + soil_row(plane, -1), N), :]
                    above = FZ[at, :]
                    total = (
                        C[at, :]
                        + FX[at, :]
                        + FX[pl.ds(base + soil_row(plane, -2), N), :]
                        + FY[at, :]
                        + FY[pl.ds(base + soil_row(plane - 1, -1), N), :]
                        + above
                        + below
                    )
                    scale = inverse(total)
                    value = B[at, :] + (above - below)
                    RD[at, :] = scale
                    B[at, :] = value
                    total = soil_sum(src, base, plane, -1, N, at, value, below, above)
                    G1[at, :] = total * scale

            @pl.loop(0, layers)
            def _(z):
                base = zbase(z)
                for plane in range(PLANES):
                    at = pl.ds(base + soil_row(plane, 0), XI)
                    below = FZ[pl.ds(base - ZP + soil_row(plane, 0), XI), :]
                    total = soil_sum(
                        G1, base, plane, 0, XI, at, B[at, :], below, FZ[at, :]
                    )
                    dst[at, :] = total * RD[at, :]

            @pl.when(p < ROUNDS - 1)
            def _():
                soil_out(other, 5 + p)
                start(soil_copies(p + 1))

        @pl.loop(0, layers)
        def _(z):
            base = zbase(z)
            for q in range(nq):
                parts = fold([BIG[H, pl.ds(base + soil_row(i, 8 * q), 8), :] for i in range(8)])
                for i in range(8):
                    NAT[z, pl.ds(i * XI + 8 * q, 8), :] = parts[i]

        out = pltpu.make_async_copy(NAT, head_out, out_sem)
        out.start()

        wait_send(soil_copies(0))
        wait_send(surface_copies(0))

        @pl.loop(1, ROUNDS)
        def _(e):
            wait_send(soil_copies(e))
            wait_send(surface_copies(e))

        sent = A_SEND.at[:, :, pl.ds(0, (n_tile - 1) * LANES)]
        pltpu.make_async_copy(sent, sent, a_send).wait()
        gone = DN.at[pl.ds(0, (n_tile - 1) * 8), :]
        pltpu.make_async_copy(gone, gone, o_send).wait()
        pltpu.make_async_copy(depth_out, depth_out, o_recv).wait()
        out.wait()

    f32 = jnp.float32

    def vmem(*shape, dtype=f32):
        return pltpu.VMEM(shape, dtype)

    wide = n_tile * LANES
    dma = pltpu.SemaphoreType.DMA
    tall = (layers + 2) * ZP
    ks, kd = 5 + ROUNDS - 1, 4 + ROUNDS - 1
    scratch = [
        vmem(6, tall, LANES),
        vmem(tall, LANES),
        vmem(tall, LANES),
        vmem(tall, LANES),
        vmem(tall, LANES),
        vmem(tall, LANES),
        vmem(tall, LANES),
        vmem(tall, LANES),
        vmem(tall, LANES),
        vmem(layers, rows, LANES),
        vmem(layers, rows, LANES, dtype=jnp.int32),
        vmem(4, 8, wide),
        vmem(4, rows, LANES),
        vmem(8, wide),
        vmem(8, wide, dtype=jnp.int32),
        vmem(rows, LANES),
        vmem(5, SP, LANES),
        vmem(SP, LANES),
        vmem(SP, LANES),
        vmem(SP, LANES),
        vmem(SP, LANES),
        vmem(SP, LANES),
        vmem(SP, LANES),
        vmem(SP, LANES),
        vmem(ks, layers, 8, LANES),
        vmem(2, ks, layers, 8, LANES),
        vmem(ks, 4, 8, LANES),
        vmem(2, ks, 4, 8, LANES),
        vmem(4, ks, 8, LANES),
        vmem(4, ks, 8, LANES),
        vmem(kd, yv, 8, LANES),
        vmem(2, kd, yv, 8, LANES),
        vmem(kd, 8, LANES),
        vmem(2, kd, 8, LANES),
        vmem(4, kd, 8, LANES),
        vmem(4, kd, 8, LANES),
        dma((7,)), dma(()), dma(()), dma(()), dma(()), dma(()),
        dma((ROUNDS, 8)), dma((ROUNDS, 8)), dma((ROUNDS, 8)), dma((ROUNDS, 8)),
    ]
    anywhere = pl.BlockSpec(memory_space=pl.ANY)
    in_vmem = pl.BlockSpec(memory_space=pltpu.VMEM)
    return pl.pallas_call(
        kernel,
        out_shape=(
            jax.ShapeDtypeStruct((layers, rows, LANES), f32),
            jax.ShapeDtypeStruct((8, wide), f32),
        ),
        in_specs=[
            anywhere, anywhere, pl.BlockSpec(memory_space=pltpu.SMEM), in_vmem, in_vmem,
            anywhere, anywhere, anywhere, anywhere, anywhere,
        ],
        out_specs=(anywhere, anywhere),
        scratch_shapes=scratch,
        compiler_params=pltpu.CompilerParams(
            collective_id=0, has_side_effects=True, vmem_limit_bytes=60 * 1024 * 1024
        ),
    )


def solution(mesh):
    n_grp, n_tile = mesh.shape["grp"], mesh.shape["tile"]

    def shards(soil_head, soil_type, soil_table, emitter_cell, emitter_rate, *surface):
        layers, rows, _ = soil_head.shape
        run = make_kernel(
            n_grp, n_tile, layers, rows, soil_table.shape[1], emitter_cell.shape[-1]
        )
        return run(soil_head, soil_type, soil_table, emitter_cell, emitter_rate, *surface)

    cells = P(None, "grp", "tile")
    strip = P(("grp", "tile"), None)
    emitters = P("grp", "tile", None)
    return jax.shard_map(
        shards,
        mesh=mesh,
        in_specs=(cells, cells, P(), emitters, emitters, strip, strip, strip, strip, strip),
        out_specs=(cells, strip),
        check_vma=False,
    )
```

profile of v0, /device:TPU:1, one launch (start us, length us, event | category | flops | bytes accessed | tf_op | source)
XLA Modules:
  0.0 82.1 jit_solution(17675187298605214017)
XLA Ops:
  0.6 78.5 %shard_map.113 = (f32[8,256,128]{2,1,0:T(8,128)}, f32[8,4096]{1,0:T(8,128)}) custom-call(f32[8,256,128]{2,1,0:T(8,128)} %head_in.1, s32[8,256,128]{2,1,0:T(8,128)} %type_in.1, f32[3,12]{1,0:T(4,128)} %table.1, s32[1,1,64]{2,1,0:T(1,128)} %cell.1, f32[1,1,64]{2,1,0:T(1,128)} %rate.1, f32[8,4096]{1,0:T(8,128)} %depth_in.1, f32[8,4096]{1,0:T(8,128)} %elev_in.1, ...), custom_call_target="tpu_custom_call" | custom-call | tf_op jit(solution)/shard_map/pallas_call | solution.py:769
  79.2 0.0 copy-start
  79.2 2.3 %copy.14 = f32[8,256,128]{2,1,0:T(8,128)} copy(f32[8,256,128]{2,1,0:T(8,128)} %get-tuple-element.4) | data formatting | bytes 2097152
  81.5 0.0 copy-done
  81.5 0.7 copy.15
Async XLA Ops:
  79.2 2.3 %copy-start = (f32[8,4096]{1,0:T(8,128)S(1)}, f32[8,4096]{1,0:T(8,128)}, u32[]{:S(2)}) copy-start(f32[8,4096]{1,0:T(8,128)} %get-tuple-element.5) | copy-start | bytes 393220
where the time goes:
time: 82.6 us; the launch traced here: 82.1 us
  Pallas kernels  78.5 us (95%)
  local copies, waits for them, and re-layouts  2.96 us (4%)
    pallas_call x1, Pallas kernels, shards(): run(soil_head, soil_type, soil_table, emitter_cell, emitter_rate, *surface)  78.5 us
    unnamed x4, local copies, waits for them, and re-layouts  2.96 us

commit v1 on v0

--- a/solution.py
+++ b/solution.py
@@ -22,8 +22,7 @@
 
 
 def inverse(x):
-    r = pl.reciprocal(x, approx=True)
-    return r * (2.0 - x * r)
+    return pl.reciprocal(x, approx=True)
 
 
 def face_of(a, b):
@@ -136,33 +135,6 @@
                         TXR[side - 2, k] = zero8
                     else:
                         TCR[side - 4, k] = zero8
-
-        for copy in loads[:5]:
-            copy.wait()
-        A_SEND[2] = ROUGH[...] * POND[...].astype(jnp.float32)
-        own = pltpu.make_async_copy(
-            A_SEND.at[:, :, pl.ds(pl.multiple_of(t * LANES, LANES), LANES)],
-            A_RECV.at[:, pl.ds(pl.multiple_of(t * 8, 8), 8), :],
-            a_recv,
-        )
-        own.start()
-
-        beside = jnp.int32(0)
-        for side in range(2, 8):
-            beside = beside + came[side].astype(jnp.int32)
-        pl.semaphore_wait(barrier, n_tile - 1 + beside)
-
-        @pl.loop(1, n_tile)
-        def _(d):
-            peer = lax.rem(t + d, n_tile)
-            pltpu.make_async_remote_copy(
-                src_ref=A_SEND.at[:, :, pl.ds(pl.multiple_of(peer * LANES, LANES), LANES)],
-                dst_ref=A_RECV.at[:, pl.ds(pl.multiple_of(t * 8, 8), 8), :],
-                send_sem=a_send,
-                recv_sem=a_recv,
-                device_id=(g, peer),
-                device_id_type=MESH,
-            ).start()
 
         def copies(bufs, k, count, send, recv):
             y_out, y_in, x_out, x_in, c_out, c_in = bufs
@@ -232,60 +204,88 @@
                         v[a | k] = jnp.where(low, roll(p, -k), q)
             return v
 
+        def zbase(z):
+            return pl.multiple_of((z + 1) * ZP, 8)
+
         def soil_row(plane, xi):
             return (plane + WS) * RP + 8 + xi
 
         def film_row(plane, xi):
             return (plane + WD) * RP + 8 + xi
 
-        def columns_out(R, base, row, width, put):
-            packed = zero8
-            for a in range(1, width + 1):
-                for q in range(nq):
-                    i = (a - 1) * nq + q
-                    high = roll(R[pl.ds(base + row(PLANES - a, 8 * q), 8), :], 8)
-                    low = roll(R[pl.ds(base + row(a - 1, 8 * q), 8), :], -8)
+        def columns_out(R, row, width, jobs):
+            spots = [(a, q) for a in range(1, width + 1) for q in range(nq)]
+            read = []
+            for base, put, values in jobs:
+                for a, q in spots:
+                    if values is None:
+                        high = R[pl.ds(base + row(PLANES - a, 8 * q), 8), :]
+                        low = R[pl.ds(base + row(a - 1, 8 * q), 8), :]
+                    else:
+                        high = values[PLANES - a][8 * q : 8 * q + 8]
+                        low = values[a - 1][8 * q : 8 * q + 8]
+                    read.append((high, low))
+            moved = [(roll(high, 8), roll(low, -8)) for high, low in read]
+            packs = []
+            for n in range(len(jobs)):
+                packed = zero8
+                for i in range(len(spots)):
+                    high, low = moved[n * len(spots) + i]
+                    both = roll(jnp.where(lane >= LANES // 2, low, high), 16 * (i % 8) + 8)
+                    packed = jnp.where(lax.shift_right_logical(lane, 4) == i % 8, both, packed)
+                    if i % 8 == 7 or i == len(spots) - 1:
+                        packs.append((n, i // 8, packed))
+                        packed = zero8
+            for n, (base, put, values) in enumerate(jobs):
+                for i, (a, q) in enumerate(spots):
+                    high, low = moved[n * len(spots) + i]
                     R[pl.ds(base + row(-a, 8 * q), 8), :] = high
                     R[pl.ds(base + row(PLANES - 1 + a, 8 * q), 8), :] = low
-                    both = jnp.where(lane >= LANES // 2, low, high)
-                    slot = i % 8
-                    moved = roll(both, 16 * slot + 8)
-                    packed = jnp.where(lax.shift_right_logical(lane, 4) == slot, moved, packed)
-                    if slot == 7 or i == width * nq - 1:
-                        put(i // 8, packed)
-                        packed = zero8
-
-        def columns_in(R, base, row, width, get):
-            for a in range(1, width + 1):
-                for q in range(nq):
-                    i = (a - 1) * nq + q
+            for n, v, packed in packs:
+                jobs[n][1](v, packed)
+
+        def columns_in(R, row, width, jobs):
+            spots = [(a, q) for a in range(1, width + 1) for q in range(nq)]
+            todo = []
+            for base, get in jobs:
+                for i, (a, q) in enumerate(spots):
                     if i % 8 == 0:
                         from_right, from_left = get(i // 8)
                         met = jnp.where(lax.bitwise_and(lane, 15) < 8, from_right, from_left)
+                    left = pl.ds(base + row(-a, 8 * q), 8)
+                    right = pl.ds(base + row(PLANES - 1 + a, 8 * q), 8)
                     u = roll(met, -(16 * (i % 8) + 8))
-                    at = pl.ds(base + row(-a, 8 * q), 8)
-                    R[at, :] = jnp.where(lane < 8, u, R[at, :])
-                    at = pl.ds(base + row(PLANES - 1 + a, 8 * q), 8)
-                    R[at, :] = jnp.where(lane >= LANES - 8, u, R[at, :])
-
-        def rows_out(R, base, row, b, slot, packed):
-            high = roll(R[pl.ds(base + row(0, XI - b), 8, stride=RP), :], 1)
-            low = roll(R[pl.ds(base + row(0, b - 1), 8, stride=RP), :], -1)
-            R[pl.ds(base + row(0, -b), 8, stride=RP), :] = high
-            R[pl.ds(base + row(0, XI - 1 + b), 8, stride=RP), :] = low
-            both = jnp.where(xb == 7, low, high)
-            mine = lax.shift_right_logical(xb, 1) == slot
-            return jnp.where(mine, roll(both, 2 * slot + 1), packed)
+                    todo.append((left, right, u, R[left, :], R[right, :]))
+            for left, right, u, was_left, was_right in todo:
+                R[left, :] = jnp.where(lane < 8, u, was_left)
+                R[right, :] = jnp.where(lane >= LANES - 8, u, was_right)
+
+        def rows_out(R, row, jobs, packs):
+            read = []
+            for base, b, slot, v in jobs:
+                high = R[pl.ds(base + row(0, XI - b), 8, stride=RP), :]
+                low = R[pl.ds(base + row(0, b - 1), 8, stride=RP), :]
+                read.append((roll(high, 1), roll(low, -1)))
+            for (base, b, slot, v), (high, low) in zip(jobs, read):
+                both = roll(jnp.where(xb == 7, low, high), 2 * slot + 1)
+                mine = lax.shift_right_logical(xb, 1) == slot
+                packs[v] = jnp.where(mine, both, packs[v])
+            for (base, b, slot, v), (high, low) in zip(jobs, read):
+                R[pl.ds(base + row(0, -b), 8, stride=RP), :] = high
+                R[pl.ds(base + row(0, XI - 1 + b), 8, stride=RP), :] = low
 
         def rows_meet(from_down, from_up):
             return jnp.where(lax.bitwise_and(lane, 1) == 1, roll(from_up, -8), roll(from_down, 8))
 
-        def rows_in(R, base, row, b, slot, met):
-            u = roll(met, -(2 * slot + 1))
-            at = pl.ds(base + row(0, -b), 8, stride=RP)
-            R[at, :] = jnp.where(xb == 0, u, R[at, :])
-            at = pl.ds(base + row(0, XI - 1 + b), 8, stride=RP)
-            R[at, :] = jnp.where(xb == 7, u, R[at, :])
+        def rows_in(R, row, jobs, met):
+            todo = []
+            for base, b, slot, v in jobs:
+                up = pl.ds(base + row(0, -b), 8, stride=RP)
+                down = pl.ds(base + row(0, XI - 1 + b), 8, stride=RP)
+                todo.append((up, down, roll(met[v], -(2 * slot + 1)), R[up, :], R[down, :]))
+            for up, down, u, was_up, was_down in todo:
+                R[up, :] = jnp.where(xb == 0, u, was_up)
+                R[down, :] = jnp.where(xb == 7, u, was_down)
 
         def corner_source(gather, side, a, b):
             plane = PLANES - a if side in (4, 6) else a - 1
@@ -312,23 +312,23 @@
         def corner_place(side, a, b):
             return -a if side in (4, 6) else PLANES - 1 + a, -b if side in (4, 5) else XI - 1 + b
 
-        def soil_out(f, k):
+        def soil_put(k, z):
+            def put(v, value):
+                YS[k, z] = value
+
+            return put
+
+        def soil_jobs(width):
+            return [
+                ((z + 1) * ZP, b, z % 4, (b - 1) * 2 + z // 4)
+                for z in range(layers)
+                for b in range(1, width + 1)
+            ]
+
+        def soil_rows_out(f, k, width):
             R = BIG.at[f]
-
-            @pl.loop(0, layers)
-            def _(z):
-                base = pl.multiple_of((z + 1) * ZP, 8)
-
-                def put(v, value):
-                    YS[k, z] = value
-
-                columns_out(R, base, soil_row, WS, put)
-
             packs = [zero8] * 4
-            for z in range(layers):
-                for b in range(1, WS + 1):
-                    v = (b - 1) * 2 + z // 4
-                    packs[v] = rows_out(R, (z + 1) * ZP, soil_row, b, z % 4, packs[v])
+            rows_out(R, soil_row, soil_jobs(width), packs)
             for v in range(4):
                 XS[k, v] = packs[v]
 
@@ -338,18 +338,21 @@
             for side in range(4, 8):
                 CS[side - 4, k] = corner_source(gather, side, 1, 1)
 
-        def soil_in(f, k):
+        def soil_in(f, k, width):
             R = BIG.at[f]
 
-            @pl.loop(0, layers)
-            def _(z):
-                base = pl.multiple_of((z + 1) * ZP, 8)
-                columns_in(R, base, soil_row, WS, lambda v: (YR[0, k, z], YR[1, k, z]))
+            @pl.loop(0, layers // 4)
+            def _(h):
+                columns_in(
+                    R, soil_row, width,
+                    [
+                        (zbase(4 * h + n), lambda v, z=4 * h + n: (YR[0, k, z], YR[1, k, z]))
+                        for n in range(4)
+                    ],
+                )
 
             met = [rows_meet(XR[0, k, v], XR[1, k, v]) for v in range(4)]
-            for z in range(layers):
-                for b in range(1, WS + 1):
-                    rows_in(R, (z + 1) * ZP, soil_row, b, z % 4, met[(b - 1) * 2 + z // 4])
+            rows_in(R, soil_row, soil_jobs(width), met)
 
             def gather(plane, xi):
                 return R[pl.ds(ZP + soil_row(plane, xi), layers, stride=ZP), :]
@@ -367,11 +370,10 @@
             def put(v, value):
                 TYS[k, v] = value
 
-            columns_out(R, 0, film_row, WD, put)
-            packed = zero8
-            for b in range(1, WD + 1):
-                packed = rows_out(R, 0, film_row, b, b - 1, packed)
-            TXS[k] = packed
+            columns_out(R, film_row, WD, [(0, put, None)])
+            packs = [zero8]
+            rows_out(R, film_row, [(0, b, b - 1, 0) for b in range(1, WD + 1)], packs)
+            TXS[k] = packs[0]
 
             def gather(plane, xi):
                 return R[pl.ds(film_row(plane, xi), 1), :]
@@ -382,10 +384,9 @@
 
         def surface_in(f, k):
             R = SF.at[f]
-            columns_in(R, 0, film_row, WD, lambda v: (TYR[0, k, v], TYR[1, k, v]))
-            met = rows_meet(TXR[0, k], TXR[1, k])
-            for b in range(1, WD + 1):
-                rows_in(R, 0, film_row, b, b - 1, met)
+            columns_in(R, film_row, WD, [(0, lambda v: (TYR[0, k, v], TYR[1, k, v]))])
+            met = [rows_meet(TXR[0, k], TXR[1, k])]
+            rows_in(R, film_row, [(0, b, b - 1, 0) for b in range(1, WD + 1)], met)
 
             def gather(plane, xi):
                 return R[pl.ds(film_row(plane, xi), 1), :]
@@ -455,43 +456,51 @@
                     at = pl.multiple_of((z + 1) * ZP + soil_row(plane, 0), 8)
                     BIG[EM, pl.ds(at, XI), :] = total[s : s + XI]
 
-        @pl.loop(0, 5)
-        def _(k):
-            soil_out(jnp.where(k == 0, 0, k + 1), k)
+        for copy in loads[:5]:
+            copy.wait()
+        A_SEND[2] = ROUGH[...] * POND[...].astype(jnp.float32)
+        own = pltpu.make_async_copy(
+            A_SEND.at[:, :, pl.ds(pl.multiple_of(t * LANES, LANES), LANES)],
+            A_RECV.at[:, pl.ds(pl.multiple_of(t * 8, 8), 8), :],
+            a_recv,
+        )
+        own.start()
+
+        beside = jnp.int32(0)
+        for side in range(2, 8):
+            beside = beside + came[side].astype(jnp.int32)
+        pl.semaphore_wait(barrier, n_tile - 1 + beside)
+
+        @pl.loop(1, n_tile)
+        def _(d):
+            peer = lax.rem(t + d, n_tile)
+            pltpu.make_async_remote_copy(
+                src_ref=A_SEND.at[:, :, pl.ds(pl.multiple_of(peer * LANES, LANES), LANES)],
+                dst_ref=A_RECV.at[:, pl.ds(pl.multiple_of(t * 8, 8), 8), :],
+                send_sem=a_send,
+                recv_sem=a_recv,
+                device_id=(g, peer),
+                device_id_type=MESH,
+            ).start()
+
+        for first, last, width in ((0, 3, WS), (3, 5, 1)):
+
+            @pl.loop(first, last)
+            def _(k):
+                field = jnp.where(k == 0, 0, k + 1)
+
+                @pl.loop(0, layers // 2)
+                def _(h):
+                    columns_out(
+                        BIG.at[field], soil_row, width,
+                        [(zbase(2 * h + n), soil_put(k, 2 * h + n), None) for n in range(2)],
+                    )
+
+                soil_rows_out(field, k, width)
 
         start(soil_copies(0))
 
-        pltpu.make_async_copy(A_RECV, A_RECV, a_recv).wait()
-
-        @pl.loop(0, 4)
-        def _(n):
-            field = jnp.where(n == 0, 0, n + 1)
-            for q in range(nq):
-                parts = fold([A_RECV[n, pl.ds(i * XI + 8 * q, 8), :] for i in range(8)])
-                for plane in range(PLANES):
-                    SF[field, pl.ds(film_row(plane, 8 * q), 8), :] = parts[plane]
-
         D, ELEV, GAIN, RAIN = 0, 2, 3, 4
-
-        @pl.loop(0, 4)
-        def _(k):
-            surface_out(jnp.where(k == 0, 0, k + 1), k)
-
-        start(surface_copies(0))
-        wait_recv(soil_copies(0))
-
-        @pl.loop(0, 5)
-        def _(k):
-            soil_in(jnp.where(k == 0, 0, k + 1), k)
-
-        wait_recv(surface_copies(0))
-
-        @pl.loop(0, 4)
-        def _(k):
-            surface_in(jnp.where(k == 0, 0, k + 1), k)
-
-        def zbase(z):
-            return pl.multiple_of((z + 1) * ZP, 8)
 
         @pl.loop(0, ROUNDS)
         def _(p):
@@ -501,24 +510,141 @@
             dst = BIG.at[other]
             depth = SF.at[slot]
 
-            @pl.when(p > 0)
-            def _():
-                wait_recv(soil_copies(p))
-                soil_in(slot, 4 + p)
-                wait_recv(surface_copies(p))
-                surface_in(slot, 3 + p)
+            def react(at, base_too):
+                grow = jnp.exp2(BIG[SHP, at, :] * jnp.minimum(src[at, :], 0.0))
+                K[at, :] = BIG[SAT, at, :] * grow
+                if base_too:
+                    store = BIG[CAP, at, :] * grow + STORAGE
+                    C[at, :] = store
+                    B[at, :] = store * BIG[H, at, :] + BIG[EM, at, :]
 
             @pl.loop(0, layers)
             def _(z):
                 base = zbase(z)
-                for plane in range(-2, PLANES + 2):
-                    at = pl.ds(base + soil_row(plane, -2), N)
-                    grow = jnp.exp2(BIG[SHP, at, :] * jnp.minimum(src[at, :], 0.0))
-                    K[at, :] = BIG[SAT, at, :] * grow
-                    if -2 < plane < PLANES + 1:
-                        store = BIG[CAP, at, :] * grow + STORAGE
-                        C[at, :] = store
-                        B[at, :] = store * BIG[H, at, :] + BIG[EM, at, :]
+                for plane in range(PLANES):
+                    react(pl.ds(base + soil_row(plane, 0), XI), True)
+
+            @pl.loop(0, layers)
+            def _(z):
+                base = zbase(z)
+                for plane in range(PLANES):
+                    at = pl.ds(base + soil_row(plane, 0), XI)
+                    k = K[at, :]
+                    FX[at, :] = face_of(k, K[pl.ds(base + soil_row(plane, 1), XI), :])
+                    FZ[at, :] = face_of(k, K[pl.ds(base + ZP + soil_row(plane, 0), XI), :])
+                    if plane < PLANES - 1:
+                        FY[at, :] = face_of(k, K[pl.ds(base + soil_row(plane + 1, 0), XI), :])
+
+            def first_at(base, plane, xi, size, stride=None):
+                def spot(dz=0, dp=0, dx=0):
+                    return pl.ds(base + dz * ZP + soil_row(plane + dp, xi + dx), size, stride=stride)
+
+                at, before, left, down = spot(), spot(dx=-1), spot(dp=-1), spot(dz=-1)
+                fx, fxm, fy, fym = FX[at, :], FX[before, :], FY[at, :], FY[left, :]
+                above, below = FZ[at, :], FZ[down, :]
+                scale = inverse(C[at, :] + fx + fxm + fy + fym + above + below)
+                RD[at, :] = scale
+                total = (
+                    B[at, :]
+                    + (above - below)
+                    + fx * src[spot(dx=1), :]
+                    + fxm * src[before, :]
+                    + fy * src[spot(dp=1), :]
+                    + fym * src[left, :]
+                    + above * src[spot(dz=1), :]
+                    + below * src[down, :]
+                )
+                G1[at, :] = total * scale
+
+            def first_outer(base):
+                for plane in (-1, 0, PLANES - 1, PLANES):
+                    first_at(base, plane, -1, N)
+                for xi in (-1, 0, XI - 1, XI):
+                    first_at(base, 0, xi, 8, RP)
+
+            @pl.loop(0, top)
+            def _(z):
+                for plane in range(1, PLANES - 1):
+                    first_at(zbase(z), plane, 0, XI)
+
+            @pl.when(p == 0)
+            def _():
+                pltpu.make_async_copy(A_RECV, A_RECV, a_recv).wait()
+
+                @pl.loop(0, 4)
+                def _(n):
+                    field = jnp.where(n == 0, 0, n + 1)
+                    for q in range(nq):
+                        parts = fold([A_RECV[n, pl.ds(i * XI + 8 * q, 8), :] for i in range(8)])
+                        for plane in range(PLANES):
+                            SF[field, pl.ds(film_row(plane, 8 * q), 8), :] = parts[plane]
+
+                @pl.loop(0, 4)
+                def _(k):
+                    surface_out(jnp.where(k == 0, 0, k + 1), k)
+
+                start(surface_copies(0))
+                wait_recv(soil_copies(0))
+
+                for first, last, width in ((0, 3, WS), (3, 5, 1)):
+
+                    @pl.loop(first, last)
+                    def _(k):
+                        soil_in(jnp.where(k == 0, 0, k + 1), k, width)
+
+            @pl.when(p > 0)
+            def _():
+                wait_recv(soil_copies(p))
+                soil_in(slot, 4 + p, WS)
+
+            def line(base, plane, xi):
+                return pl.ds(base + soil_row(plane, xi), 8, stride=RP)
+
+            @pl.loop(0, layers)
+            def _(z):
+                base = zbase(z)
+                for plane in (-2, -1, PLANES, PLANES + 1):
+                    react(pl.ds(base + soil_row(plane, -2), N), plane in (-1, PLANES))
+                for xi in (-2, -1, XI, XI + 1):
+                    react(line(base, 0, xi), xi in (-1, XI))
+
+            @pl.loop(0, layers)
+            def _(z):
+                base = zbase(z)
+                for plane in (-2, -1, PLANES - 1, PLANES):
+                    at = pl.ds(base + soil_row(plane, -1), N)
+                    k = K[at, :]
+                    FY[at, :] = face_of(k, K[pl.ds(base + soil_row(plane + 1, -1), N), :])
+                    if plane in (-1, PLANES):
+                        FZ[at, :] = face_of(k, K[pl.ds(base + ZP + soil_row(plane, -1), N), :])
+                        before = pl.ds(base + soil_row(plane, -2), N)
+                        FX[before, :] = face_of(K[before, :], k)
+                for xi in (-2, -1, XI - 1, XI):
+                    at = line(base, 0, xi)
+                    k = K[at, :]
+                    FX[at, :] = face_of(k, K[line(base, 0, xi + 1), :])
+                    if xi in (-1, XI):
+                        FZ[at, :] = face_of(k, K[line(base + ZP, 0, xi), :])
+                        FY[at, :] = face_of(k, K[line(base, 1, xi), :])
+
+            early = jnp.where(p < ROUNDS - 1, top, 0)
+
+            @pl.loop(0, early)
+            def _(z):
+                first_outer(zbase(z))
+
+            @pl.when(p == 0)
+            def _():
+                wait_recv(surface_copies(0))
+
+                @pl.loop(0, 4)
+                def _(k):
+                    surface_in(jnp.where(k == 0, 0, k + 1), k)
+
+            @pl.when(p > 0)
+            def _():
+                wait_recv(surface_copies(p))
+                surface_in(slot, 3 + p)
 
             for plane in range(-3, PLANES + 3):
                 at = pl.ds(film_row(plane, -3), N)
@@ -597,18 +723,6 @@
                         device_id_type=MESH,
                     ).start()
 
-            @pl.loop(0, layers)
-            def _(z):
-                base = zbase(z)
-                for plane in range(-2, PLANES + 1):
-                    at = pl.ds(base + soil_row(plane, -1), N)
-                    k = K[at, :]
-                    FY[at, :] = face_of(k, K[pl.ds(base + soil_row(plane + 1, -1), N), :])
-                    if plane > -2:
-                        FZ[at, :] = face_of(k, K[pl.ds(base + ZP + soil_row(plane, -1), N), :])
-                        before = pl.ds(base + soil_row(plane, -2), N)
-                        FX[before, :] = face_of(K[before, :], k)
-
             def soil_sum(source, base, plane, first, size, at, value, below, above):
                 after = pl.ds(base + soil_row(plane, first + 1), size)
                 before = pl.ds(base + soil_row(plane, first - 1), size)
@@ -624,55 +738,47 @@
                     + below * source[pl.ds(base - ZP + soil_row(plane, first), size), :]
                 )
 
-            @pl.loop(0, layers)
+            @pl.loop(early, top)
             def _(z):
-                base = zbase(z)
-                for plane in range(-1, PLANES + 1):
-                    at = pl.ds(base + soil_row(plane, -1), N)
-                    below = FZ[pl.ds(base - ZP + soil_row(plane, -1), N), :]
-                    above = FZ[at, :]
-                    total = (
-                        C[at, :]
-                        + FX[at, :]
-                        + FX[pl.ds(base + soil_row(plane, -2), N), :]
-                        + FY[at, :]
-                        + FY[pl.ds(base + soil_row(plane - 1, -1), N), :]
-                        + above
-                        + below
-                    )
-                    scale = inverse(total)
-                    value = B[at, :] + (above - below)
-                    RD[at, :] = scale
-                    B[at, :] = value
-                    total = soil_sum(src, base, plane, -1, N, at, value, below, above)
-                    G1[at, :] = total * scale
-
-            @pl.loop(0, layers)
-            def _(z):
-                base = zbase(z)
+                first_outer(zbase(z))
+
+            for plane in range(-1, PLANES + 1):
+                first_at(high, plane, -1, N)
+
+            def second_sweep(base):
+                values = []
                 for plane in range(PLANES):
                     at = pl.ds(base + soil_row(plane, 0), XI)
                     below = FZ[pl.ds(base - ZP + soil_row(plane, 0), XI), :]
                     total = soil_sum(
-                        G1, base, plane, 0, XI, at, B[at, :], below, FZ[at, :]
+                        G1, base, plane, 0, XI, at, B[at, :] + (FZ[at, :] - below), below, FZ[at, :]
                     )
-                    dst[at, :] = total * RD[at, :]
+                    values.append(total * RD[at, :])
+                    dst[at, :] = values[-1]
+                return values
 
             @pl.when(p < ROUNDS - 1)
             def _():
-                soil_out(other, 5 + p)
+                @pl.loop(0, layers)
+                def _(z):
+                    base = zbase(z)
+                    values = second_sweep(base)
+                    columns_out(dst, soil_row, WS, [(base, soil_put(5 + p, z), values)])
+
+                soil_rows_out(other, 5 + p, WS)
                 start(soil_copies(p + 1))
 
-        @pl.loop(0, layers)
-        def _(z):
-            base = zbase(z)
-            for q in range(nq):
-                parts = fold([BIG[H, pl.ds(base + soil_row(i, 8 * q), 8), :] for i in range(8)])
-                for i in range(8):
-                    NAT[z, pl.ds(i * XI + 8 * q, 8), :] = parts[i]
-
-        out = pltpu.make_async_copy(NAT, head_out, out_sem)
-        out.start()
+            @pl.when(p == ROUNDS - 1)
+            def _():
+                @pl.loop(0, layers)
+                def _(z):
+                    base = zbase(z)
+                    values = second_sweep(base)
+                    for q in range(nq):
+                        parts = fold([values[i][8 * q : 8 * q + 8] for i in range(8)])
+                        for i in range(8):
+                            NAT[z, pl.ds(i * XI + 8 * q, 8), :] = parts[i]
+                    pltpu.make_async_copy(NAT.at[z], head_out.at[z], out_sem).start()
 
         wait_send(soil_copies(0))
         wait_send(surface_copies(0))
@@ -687,7 +793,7 @@
         gone = DN.at[pl.ds(0, (n_tile - 1) * 8), :]
         pltpu.make_async_copy(gone, gone, o_send).wait()
         pltpu.make_async_copy(depth_out, depth_out, o_recv).wait()
-        out.wait()
+        pltpu.make_async_copy(NAT, head_out, out_sem).wait()
 
     f32 = jnp.float32
 

time: 82.6 us -> 71.4 us (0.86)
  Pallas kernels: 78.5 us -> 67.6 us
    pallas_call x1, Pallas kernels: 78.5 us -> 67.6 us  [shards(): run(soil_head, soil_type, soil_table, emitter_cell, emitter_rate, *surface)]
where the time goes in v1:
time: 71.4 us; the launch traced here: 71.2 us
  Pallas kernels  67.6 us (95%)
  local copies, waits for them, and re-layouts  2.96 us (4%)
    pallas_call x1, Pallas kernels, shards(): run(soil_head, soil_type, soil_table, emitter_cell, emitter_rate, *surface)  67.6 us
    unnamed x4, local copies, waits for them, and re-layouts  2.96 us

profile of v1, /device:TPU:1, one launch (start us, length us, event | category | flops | bytes accessed | tf_op | source)
XLA Modules:
  0.0 71.2 jit_solution(2274522700495210611)
XLA Ops:
  0.6 67.6 %shard_map.113 = (f32[8,256,128]{2,1,0:T(8,128)}, f32[8,4096]{1,0:T(8,128)}) custom-call(f32[8,256,128]{2,1,0:T(8,128)} %head_in.1, s32[8,256,128]{2,1,0:T(8,128)} %type_in.1, f32[3,12]{1,0:T(4,128)} %table.1, s32[1,1,64]{2,1,0:T(1,128)} %cell.1, f32[1,1,64]{2,1,0:T(1,128)} %rate.1, f32[8,4096]{1,0:T(8,128)} %depth_in.1, f32[8,4096]{1,0:T(8,128)} %elev_in.1, ...), custom_call_target="tpu_custom_call" | custom-call | tf_op jit(solution)/shard_map/pallas_call | solution.py:875
  68.3 0.0 copy-start
  68.3 2.3 %copy.14 = f32[8,256,128]{2,1,0:T(8,128)} copy(f32[8,256,128]{2,1,0:T(8,128)} %get-tuple-element.4) | data formatting | bytes 2097152
  70.6 0.0 copy-done
  70.6 0.7 copy.15
Async XLA Ops:
  68.3 2.3 %copy-start = (f32[8,4096]{1,0:T(8,128)S(1)}, f32[8,4096]{1,0:T(8,128)}, u32[]{:S(2)}) copy-start(f32[8,4096]{1,0:T(8,128)} %get-tuple-element.5) | copy-start | bytes 393220

commit v2 on v1

--- a/solution.py
+++ b/solution.py
@@ -1,3 +1,5 @@
+import functools
+
 import jax
 import jax.numpy as jnp
 from jax import lax
@@ -148,7 +150,8 @@
                 else:
                     src, dst = c_out.at[side - 4, at], c_in.at[side - 4, at]
                 out.append(
-                    pltpu.make_async_remote_copy(
+                    functools.partial(
+                        pltpu.make_async_remote_copy,
                         src_ref=src,
                         dst_ref=dst,
                         send_sem=send.at[side],
@@ -172,26 +175,26 @@
                 return copies(surface_bufs, 0, 4, t_send.at[0], t_recv.at[0])
             return copies(surface_bufs, 3 + e, 1, t_send.at[e], t_recv.at[e])
 
-        def start(made):
-            for side in (1, 0, 4, 5, 6, 7, 2, 3):
+        def start(made, sides=(4, 5, 6, 7, 1, 0, 2, 3)):
+            for side in sides:
 
                 @pl.when(has[side])
                 def _():
-                    made[side].start()
-
-        def wait_recv(made):
-            for side in range(8):
+                    made[side]().start()
+
+        def wait_recv(made, sides=range(8)):
+            for side in sides:
 
                 @pl.when(came[side])
                 def _():
-                    made[side].wait_recv()
+                    made[side]().wait_recv()
 
         def wait_send(made):
             for side in range(8):
 
                 @pl.when(has[side])
                 def _():
-                    made[side].wait_send()
+                    made[side]().wait_send()
 
         def fold(v):
             v = list(v)
@@ -325,42 +328,45 @@
                 for b in range(1, width + 1)
             ]
 
+        def soil_gather(R):
+            def gather(plane, xi):
+                return R[pl.ds(ZP + soil_row(plane, xi), layers, stride=ZP), :]
+
+            return gather
+
+        def soil_corners_out(f, k):
+            for side in range(4, 8):
+                CS[side - 4, k] = corner_source(soil_gather(BIG.at[f]), side, 1, 1)
+
         def soil_rows_out(f, k, width):
-            R = BIG.at[f]
             packs = [zero8] * 4
-            rows_out(R, soil_row, soil_jobs(width), packs)
+            rows_out(BIG.at[f], soil_row, soil_jobs(width), packs)
             for v in range(4):
                 XS[k, v] = packs[v]
 
-            def gather(plane, xi):
-                return R[pl.ds(ZP + soil_row(plane, xi), layers, stride=ZP), :]
-
-            for side in range(4, 8):
-                CS[side - 4, k] = corner_source(gather, side, 1, 1)
-
-        def soil_in(f, k, width):
-            R = BIG.at[f]
-
+        def soil_rows_in(f, k, width):
+            met = [rows_meet(XR[0, k, v], XR[1, k, v]) for v in range(4)]
+            rows_in(BIG.at[f], soil_row, soil_jobs(width), met)
+
+        def soil_columns_in(f, k, width):
             @pl.loop(0, layers // 4)
             def _(h):
                 columns_in(
-                    R, soil_row, width,
+                    BIG.at[f], soil_row, width,
                     [
                         (zbase(4 * h + n), lambda v, z=4 * h + n: (YR[0, k, z], YR[1, k, z]))
                         for n in range(4)
                     ],
                 )
 
-            met = [rows_meet(XR[0, k, v], XR[1, k, v]) for v in range(4)]
-            rows_in(R, soil_row, soil_jobs(width), met)
-
-            def gather(plane, xi):
-                return R[pl.ds(ZP + soil_row(plane, xi), layers, stride=ZP), :]
-
+        def soil_corners_in(f, k):
+            R = BIG.at[f]
+            values = [
+                corner_value(soil_gather(R), side, 1, 1, CR[side - 4, k]) for side in range(4, 8)
+            ]
             for side in range(4, 8):
-                value = corner_value(gather, side, 1, 1, CR[side - 4, k])
                 plane, xi = corner_place(side, 1, 1)
-                R[pl.ds(ZP + soil_row(plane, xi), layers, stride=ZP), :] = value
+                R[pl.ds(ZP + soil_row(plane, xi), layers, stride=ZP), :] = values[side - 4]
 
         corners = ((1, 1), (1, 2), (2, 1))
 
@@ -496,6 +502,7 @@
                         [(zbase(2 * h + n), soil_put(k, 2 * h + n), None) for n in range(2)],
                     )
 
+                soil_corners_out(field, k)
                 soil_rows_out(field, k, width)
 
         start(soil_copies(0))
@@ -590,27 +597,36 @@
 
                     @pl.loop(first, last)
                     def _(k):
-                        soil_in(jnp.where(k == 0, 0, k + 1), k, width)
+                        field = jnp.where(k == 0, 0, k + 1)
+                        soil_rows_in(field, k, width)
+                        soil_columns_in(field, k, width)
+                        soil_corners_in(field, k)
 
             @pl.when(p > 0)
             def _():
-                wait_recv(soil_copies(p))
-                soil_in(slot, 4 + p, WS)
+                wait_recv(soil_copies(p), (2, 3))
+                soil_rows_in(slot, 4 + p, WS)
+                wait_recv(soil_copies(p), (0, 1))
+                soil_columns_in(slot, 4 + p, WS)
+                wait_recv(soil_copies(p), (4, 5, 6, 7))
+                soil_corners_in(slot, 4 + p)
 
             def line(base, plane, xi):
                 return pl.ds(base + soil_row(plane, xi), 8, stride=RP)
 
-            @pl.loop(0, layers)
-            def _(z):
-                base = zbase(z)
+            def outer_react(base):
                 for plane in (-2, -1, PLANES, PLANES + 1):
                     react(pl.ds(base + soil_row(plane, -2), N), plane in (-1, PLANES))
                 for xi in (-2, -1, XI, XI + 1):
                     react(line(base, 0, xi), xi in (-1, XI))
 
-            @pl.loop(0, layers)
+            last = p == ROUNDS - 1
+
+            @pl.loop(jnp.where(last, top, 0), layers)
             def _(z):
-                base = zbase(z)
+                outer_react(zbase(z))
+
+            def outer_faces(base):
                 for plane in (-2, -1, PLANES - 1, PLANES):
                     at = pl.ds(base + soil_row(plane, -1), N)
                     k = K[at, :]
@@ -626,6 +642,10 @@
                     if xi in (-1, XI):
                         FZ[at, :] = face_of(k, K[line(base + ZP, 0, xi), :])
                         FY[at, :] = face_of(k, K[line(base, 1, xi), :])
+
+            @pl.loop(0, jnp.where(p < ROUNDS - 1, layers, 0))
+            def _(z):
+                outer_faces(zbase(z))
 
             early = jnp.where(p < ROUNDS - 1, top, 0)
 
@@ -738,6 +758,14 @@
                     + below * source[pl.ds(base - ZP + soil_row(plane, first), size), :]
                 )
 
+            @pl.loop(0, jnp.where(last, top, 0))
+            def _(z):
+                outer_react(zbase(z))
+
+            @pl.loop(jnp.where(p < ROUNDS - 1, layers, 0), layers)
+            def _(z):
+                outer_faces(zbase(z))
+
             @pl.loop(early, top)
             def _(z):
                 first_outer(zbase(z))
@@ -765,8 +793,10 @@
                     values = second_sweep(base)
                     columns_out(dst, soil_row, WS, [(base, soil_put(5 + p, z), values)])
 
+                soil_corners_out(other, 5 + p)
+                start(soil_copies(p + 1), (4, 5, 6, 7, 1, 0))
                 soil_rows_out(other, 5 + p, WS)
-                start(soil_copies(p + 1))
+                start(soil_copies(p + 1), (2, 3))
 
             @pl.when(p == ROUNDS - 1)
             def _():

time: 71.4 us -> 70.3 us (0.985)
  Pallas kernels: 67.6 us -> 66.4 us
    pallas_call x1, Pallas kernels: 67.6 us -> 66.4 us  [shards(): run(soil_head, soil_type, soil_table, emitter_cell, emitter_rate, *surface)]
where the time goes in v2:
time: 70.3 us; the launch traced here: 70 us
  Pallas kernels  66.4 us (94%)
  local copies, waits for them, and re-layouts  2.96 us (4%)
    pallas_call x1, Pallas kernels, shards(): run(soil_head, soil_type, soil_table, emitter_cell, emitter_rate, *surface)  66.4 us
    unnamed x4, local copies, waits for them, and re-layouts  2.96 us

profile of v2, /device:TPU:1, one launch (start us, length us, event | category | flops | bytes accessed | tf_op | source)
XLA Modules:
  0.0 70.0 jit_solution(10812690316356261398)
XLA Ops:
  0.6 66.4 %shard_map.113 = (f32[8,256,128]{2,1,0:T(8,128)}, f32[8,4096]{1,0:T(8,128)}) custom-call(f32[8,256,128]{2,1,0:T(8,128)} %head_in.1, s32[8,256,128]{2,1,0:T(8,128)} %type_in.1, f32[3,12]{1,0:T(4,128)} %table.1, s32[1,1,64]{2,1,0:T(1,128)} %cell.1, f32[1,1,64]{2,1,0:T(1,128)} %rate.1, f32[8,4096]{1,0:T(8,128)} %depth_in.1, f32[8,4096]{1,0:T(8,128)} %elev_in.1, ...), custom_call_target="tpu_custom_call" | custom-call | tf_op jit(solution)/shard_map/pallas_call | solution.py:905
  67.1 0.0 copy-start
  67.1 2.3 %copy.14 = f32[8,256,128]{2,1,0:T(8,128)} copy(f32[8,256,128]{2,1,0:T(8,128)} %get-tuple-element.4) | data formatting | bytes 2097152
  69.4 0.0 copy-done
  69.4 0.7 copy.15
Async XLA Ops:
  67.1 2.3 %copy-start = (f32[8,4096]{1,0:T(8,128)S(1)}, f32[8,4096]{1,0:T(8,128)}, u32[]{:S(2)}) copy-start(f32[8,4096]{1,0:T(8,128)} %get-tuple-element.5) | copy-start | bytes 393220
